TPU v7x, 32 devices: a whole 2x2x4 slice. The times are simulated.
32 devices in a mesh: row: 4 (over y, core), col: 8 (over z, x).
Axes of the slice: x: 2, y: 2, z: 4, core: 2. Of those that a mesh axis runs over, the one named last changes fastest.
Arguments:
- occ_coeffs: bfloat16 [49152, 20480], P('row', 'col'), may hold values from -0.21875 to 0.21875
- colloc: bfloat16 [256, 1024, 512], P(('row', 'col')), may hold values from -6 to 6
- grid_points: float32 [256, 3, 512], P(('row', 'col')), may hold values from -4 to 4
- grid_weights: float32 [256, 512], P(('row', 'col')), may hold values from 0.01 to 0.1
- charge_sites: float32 [3, 512], replicated, may hold values from -4 to 4
- charge_proj: bfloat16 [512, 128], replicated, may hold values from -0.5 to 0.5
- shell_lists: int32 [256, 16], P(('row', 'col')), may hold values from 0 to 767, as said below
- point_counts: int32 [256], P(('row', 'col')), may hold values from 1 to 512, as said below
Outputs:
- exchange_slab: float32 [49152, 128], P(('row', 'col'))
Inputs may be any that keep to these rules, and one draw needn't show every extreme that they name: `shell_lists`: batches b * 8 to b * 8 + 7 belong to the b-th device in row+col order, and the blocks named by one device's batches are all different. Owner device o holds blocks o * 24 to o * 24 + 23; one device's batches name at most 8 blocks of one owner, and in every draw one owner gets exactly 8 from every device. `point_counts`: points of a batch beyond its count are not part of it.
All inputs are finite; a program needn't handle non-finite values.
Results may differ from a plain program's by a relative error of at most 0.0045.
Values may be sent and summed in bfloat16 or wider, within the bound.
A program may use at most 128 MiB of HBM per device.

v0:
```python
import jax
import jax.numpy as jnp
from jax import lax
from jax.sharding import PartitionSpec as P

SH = 64
NSIG = 16


smear_sq = 0.25


def from_root(value, axis, source):
    kept = jnp.where(lax.axis_index(axis) == source, value, 0).astype(value.dtype)
    return lax.psum(kept, axis)


def potential(points, charge_sites):
    dist_sq = (points[0][None, :] - charge_sites[0][:, None]) ** 2
    dist_sq = dist_sq + (points[1][None, :] - charge_sites[1][:, None]) ** 2
    dist_sq = dist_sq + (points[2][None, :] - charge_sites[2][:, None]) ** 2
    return lax.rsqrt(dist_sq + smear_sq)


def batch_terms(
    dens_rows, colloc, grid_points, grid_weights, charge_sites, charge_proj, point_counts
):
    slab_width = charge_proj.shape[1]
    total_points = colloc.shape[2]
    block_points = min(256, total_points)
    func_rows = colloc.shape[1]

    def one_batch(carry, item):
        batch_rows, batch_colloc, batch_points, batch_weights, count = item
        blocks_used = (count + block_points - 1) // block_points

        def point_block(index, accumulated):
            start = index * block_points
            values = lax.dynamic_slice_in_dim(batch_colloc, start, block_points, 1)
            points = lax.dynamic_slice_in_dim(batch_points, start, block_points, 1)
            weights = lax.dynamic_slice_in_dim(batch_weights, start, block_points, 0)
            live = (start + jnp.arange(block_points) < count).astype(jnp.float32)
            field = lax.dot_general(
                batch_rows, values, (((0,), (0,)), ((), ())), preferred_element_type=jnp.float32
            ).astype(jnp.bfloat16)
            projected = jnp.dot(charge_proj, field, preferred_element_type=jnp.float32)
            charges = (
                projected * potential(points, charge_sites) * (weights * live)[None, :]
            ).astype(jnp.bfloat16)
            spread_back = lax.dot_general(
                charge_proj, charges, (((0,), (0,)), ((), ())), preferred_element_type=jnp.float32
            ).astype(jnp.bfloat16)
            return accumulated + lax.dot_general(
                values, spread_back, (((1,), (1,)), ((), ())), preferred_element_type=jnp.float32
            )

        start_value = jnp.zeros((func_rows, slab_width), jnp.float32)
        return (carry, lax.fori_loop(0, blocks_used, point_block, start_value))

    _, terms = lax.scan(one_batch, 0, (dens_rows, colloc, grid_points, grid_weights, point_counts))
    return terms


def on_device(
    occ_coeffs,
    colloc,
    grid_points,
    grid_weights,
    charge_sites,
    charge_proj,
    shell_lists,
    point_counts,
):
    row_count = lax.axis_size("row")
    col_count = lax.axis_size("col")
    owners = row_count * col_count
    group_rows = occ_coeffs.shape[0]
    slab_width = charge_proj.shape[1]
    own_rows = group_rows // col_count
    own_blocks = own_rows // SH
    window = from_root(occ_coeffs[:slab_width], "row", 0)
    requested = shell_lists.reshape(-1)
    request_count = requested.shape[0]
    capacity = 2 * request_count // owners
    owner = requested // own_blocks
    onehot = (owner[:, None] == jnp.arange(owners)[None, :]).astype(jnp.int32)
    before = jnp.cumsum(onehot, axis=0) - onehot
    rank = jnp.sum(before * onehot, axis=1)
    slot = owner * capacity + rank
    empty_ids = jnp.full((owners * capacity,), -1, jnp.int32)
    density = lax.psum_scatter(
        lax.dot_general(
            occ_coeffs, window, (((1,), (1,)), ((), ())), preferred_element_type=jnp.float32
        ),
        "col",
        scatter_dimension=0,
        tiled=True,
    ).astype(jnp.bfloat16)
    store = density.reshape(own_blocks, SH, slab_width)
    wanted = empty_ids.at[slot].set(requested % own_blocks).reshape(owners, capacity)
    received_ids = lax.all_to_all(wanted, ("row", "col"), split_axis=0, concat_axis=0, tiled=True)
    found = store[jnp.maximum(received_ids, 0)]
    replies, received_ids = (
        lax.all_to_all(found, ("row", "col"), split_axis=0, concat_axis=0, tiled=True),
        received_ids,
    )
    fetched = replies.reshape(owners * capacity, SH, slab_width)[slot]
    dens_rows = fetched.reshape(shell_lists.shape[0], NSIG * SH, slab_width)
    terms = batch_terms(
        dens_rows, colloc, grid_points, grid_weights, charge_sites, charge_proj, point_counts
    )
    tiles = (
        jnp.zeros((owners * capacity, SH, slab_width), jnp.float32)
        .at[slot]
        .set(terms.reshape(request_count, SH, slab_width))
    )
    tiles = tiles.reshape(wanted.shape + (SH, slab_width))
    arrived = lax.all_to_all(tiles, ("row", "col"), split_axis=0, concat_axis=0, tiled=True)
    flat_ids = received_ids.reshape(-1)
    selector = (jnp.arange(store.shape[0])[:, None] == flat_ids[None, :]).astype(jnp.float32)
    summed = jnp.dot(
        selector,
        arrived.reshape(flat_ids.shape[0], SH * slab_width),
        precision=lax.Precision.HIGHEST,
        preferred_element_type=jnp.float32,
    )
    return summed.reshape(own_rows, slab_width)


def solution(mesh):
    placed = (
        P("row", "col"),
        P(("row", "col"), None, None),
        P(("row", "col"), None, None),
        P(("row", "col"), None),
        P(),
        P(),
        P(("row", "col"), None),
        P(("row", "col")),
    )
    return jax.shard_map(
        on_device, mesh=mesh, in_specs=placed, out_specs=P(("row", "col"), None), check_vma=False
    )
```

profile of v0, /device:TPU:12, one launch (start us, length us, event | category | flops | bytes accessed | tf_op | source)
XLA Modules:
  0.0 599.3 jit_solution(9642797417430150663)
XLA Ops:
  6.5 2.0 slice_select_fusion
  8.6 35.1 %all-reduce.2.cloned.1.call-done = bf16[128,2560]{1,0:T(8,128)(2,1)} async-done(((bf16[128,2560]{1,0:T(8,128)(2,1)}), bf16[128,2560]{1,0:T(8,128)(2,1)}) %all-reduce.2.cloned.1.call-update) | async-done | bytes 655376 | tf_op jit(solution)/shard_map/psum | solution.py:15
  43.7 28.3 %convolution_bitcast_fusion.1 = f32[12288,128]{0,1:T(8,128)} fusion(bf16[128,2560]{1,0:T(8,128)(2,1)} %all-reduce.2.cloned.1.call-done, bf16[12288,2560]{1,0:T(8,128)(2,1)} %param.12), kind=kOutput, calls=%fused_computation.43 | convolution fusion | flops 8053063680 | bytes 69861376 | tf_op jit(solution)/shard_map/dot_general | solution.py:92
  74.6 10.7 %all_to_all.19 = s32[32,1,8]{2,1,0:T(1,128)S(1)} all-to-all(s32[32,1,8]{2,1,0:T(1,128)S(1)} %bitcast.106), channel_id=1, replica_groups=mesh['row'=4,'col'=8] {'row','col'}, dimensions={0} | all-to-all | bytes 2048 | tf_op jit(solution)/shard_map/all_to_all | solution.py:101
  86.7 104.1 %reduce-scatter.2.cloned.1.call-done = f32[1536,128]{0,1:T(8,128)} async-done(((f32[12288,128]{0,1:T(8,128)}), f32[1536,128]{0,1:T(8,128)}) %reduce-scatter.2.cloned.1.call-update) | async-done | bytes 786448 | tf_op jit(solution)/shard_map/reduce_scatter | solution.py:91
  192.2 3.1 gather_fusion
  195.2 4.8 all-to-all-start.1
  200.1 91.0 %all-to-all-done.1 = bf16[32,8,64,128]{3,2,1,0:T(8,128)(2,1)} async-done(((bf16[32,8,64,128]{3,2,1,0:T(8,128)(2,1)}), bf16[32,8,64,128]{3,2,1,0:T(8,128)(2,1)}, u32[]{:S(2)}, u32[]{:S(2)}) %all-to-all-start.1) | async-done | bytes 4194336 | tf_op jit(solution)/shard_map/all_to_all | solution.py:104
  291.2 4.3 gather_fusion.1
  295.5 69.3 %while.47 = (s32[]{:T(128)}, f32[8,1024,128]{2,1,0:T(8,128)}, s32[8]{0:T(128)S(1)}, bf16[8,1024,512]{2,1,0:T(8,128)(2,1)}, f32[8,3,512]{2,0,1:T(8,128)}, /*index...) while((s32[]{:T(128)}, f32[8,1024,128]{2,1,0:T(8,128)}, ...), condition=%wide.region_8.9_spmd, body=%wide.region_5.8_spmd.sunk | while | flops 203096848 | bytes 7007006 | solution.py:60
  300.6 1.9 while.48
  308.6 3.9 while.48
  318.5 3.9 while.48
  328.4 1.9 while.48
  334.9 1.3 dynamic-slice_bitcast_fusion.4
  336.3 1.9 while.48
  344.2 1.9 while.48
  352.2 1.9 while.48
  360.1 3.9 while.48
  364.8 4.3 broadcast_in_dim.33
  369.1 19.6 %scatter_fusion = f32[256,64,128]{2,1,0:T(8,128)} fusion(f32[256,64,128]{2,1,0:T(8,128)} %broadcast_in_dim.33, s32[128]{0:T(128)S(1)} %fusion.35, f32[128,64,128]{2,1,0:T(8,128)} %bitcast.97), kind=kCustom, calls=%fused_computation.3 | custom fusion | bytes 12583424 | tf_op jit(solution)/shard_map/scatter | solution.py:115
  388.7 9.8 %all-to-all-start.2 = ((f32[32,8,64,128]{3,2,1,0:T(8,128)}), f32[32,8,64,128]{3,2,1,0:T(8,128)}, u32[]{:S(2)}, u32[]{:S(2)}) async-start(f32[32,8,64,128]{3,2,1,0:T(8,128)} %bitcast.95), calls=%async_computation.3 | async-start | bytes 16777216 | tf_op jit(solution)/shard_map/all_to_all | solution.py:118
  398.6 182.5 %all-to-all-done.2 = f32[32,8,64,128]{3,2,1,0:T(8,128)} async-done(((f32[32,8,64,128]{3,2,1,0:T(8,128)}), f32[32,8,64,128]{3,2,1,0:T(8,128)}, u32[]{:S(2)}, u32[]{:S(2)}) %all-to-all-start.2) | async-done | bytes 8388640 | tf_op jit(solution)/shard_map/all_to_all | solution.py:118
  581.0 10.4 %fusion.28 = f32[24,8192]{1,0:T(8,128)S(1)} fusion(f32[32,8,64,128]{3,2,1,0:T(8,128)} %all-to-all-done.2, s32[256]{0:T(256)S(1)} %eq.37), kind=kOutput, calls=%fused_computation.44 | convolution fusion | flops 603985920 | bytes 9176064 | tf_op jit(solution)/shard_map/dot_general | solution.py:121
  (165 shorter events, 68.5 us)
Async XLA Ops:
  6.5 37.1 %all-reduce.2.cloned.1.call-start = ((), (), s32[]{:S(2)}) async-start(), calls=%async_computation.4 | async-start | bytes 1310720 | tf_op jit(solution)/shard_map/psum | solution.py:15
  8.5 182.2 %reduce-scatter.2.cloned.1.call-start = ((), (), s32[]{:S(2)}) async-start(), calls=%async_computation.5 | async-start | bytes 7077888 | tf_op jit(solution)/shard_map/reduce_scatter | solution.py:91
  72.0 0.7 copy-start.1
  195.2 95.9 %all-to-all-start.1 = ((bf16[32,8,64,128]{3,2,1,0:T(8,128)(2,1)}), bf16[32,8,64,128]{3,2,1,0:T(8,128)(2,1)}, u32[]{:S(2)}, u32[]{:S(2)}) async-start(bf16[32,8,64,128]{3,2,1,0:T(8,128)(2,1)} %bitcast.96), calls=%async_computation.2 | async-start | bytes 8388608 | tf_op jit(solution)/shard_map/all_to_all | solution.py:104
  200.1 95.4 %copy-start = (f32[3,512]{1,0:T(4,128)S(1)}, f32[3,512]{1,0:T(4,128)}, u32[]{:S(2)}) copy-start(f32[3,512]{1,0:T(4,128)} %param.16) | copy-start | bytes 18436
  200.1 95.4 %copy-start.2 = (bf16[512,128]{1,0:T(8,128)(2,1)S(1)}, bf16[512,128]{1,0:T(8,128)(2,1)}, u32[]{:S(2)}) copy-start(bf16[512,128]{1,0:T(8,128)(2,1)} %param.17) | copy-start | bytes 393220
  200.1 95.4 %copy-start.3 = (s32[8]{0:T(128)S(1)}, s32[8]{0:T(128)}, u32[]{:S(2)}) copy-start(s32[8]{0:T(128)} %param.19) | copy-start | bytes 100
  388.7 192.4 %all-to-all-start.2 = ((f32[32,8,64,128]{3,2,1,0:T(8,128)}), f32[32,8,64,128]{3,2,1,0:T(8,128)}, u32[]{:S(2)}, u32[]{:S(2)}) async-start(f32[32,8,64,128]{3,2,1,0:T(8,128)} %bitcast.95), calls=%async_computation.3 | async-start | bytes 16777216 | tf_op jit(solution)/shard_map/all_to_all | solution.py:118
Sparse Core Ops, SparseCore 0:
  9.7 33.9 all-reduce.1
  72.1 118.5 reduce-scatter.1
where the time goes:
time: 608 us; the launch traced here: 599 us
  waiting for transfers between devices  413 us (68%)
  local copies, waits for them, and re-layouts  78.7 us (13%)
  matrix products  50.8 us (8%)
  starting transfers between devices  14.7 us (2%)
  between operations  13.5 us (2%)
  other arithmetic  12.2 us (2%)
  blocking collectives  10.7 us (2%)
    all_to_all x1, waiting for transfers between devices, on_device(): lax.all_to_all(tiles, ('row', 'col'), split_axis=0, concat_axis=0, tiled=...  182 us
    reduce_scatter x1, waiting for transfers between devices, on_device(): lax.psum_scatter(lax.dot_general(occ_coeffs, window, (((1,), (1,)), ((),...  104 us
    all_to_all x1, waiting for transfers between devices, on_device(): lax.all_to_all(found, ('row', 'col'), split_axis=0, concat_axis=0, tiled=...  91 us
    psum x1, waiting for transfers between devices, from_root(): return lax.psum(kept, axis)  35.1 us
    dot_general x1, matrix products, on_device(): lax.dot_general(occ_coeffs, window, (((1,), (1,)), ((), ())), preferred_e...  28.3 us
    scatter x1, local copies, waits for them, and re-layouts, on_device(): tiles = jnp.zeros((owners * capacity, SH, slab_width), jnp.float32).at[sl...  19.6 us
    squeeze x16, local copies, waits for them, and re-layouts, batch_terms(): lax.scan(one_batch, 0, (dens_rows, colloc, grid_points, grid_weights, poi...  18.2 us
    dynamic_slice x32, local copies, waits for them, and re-layouts, batch_terms(): lax.scan(one_batch, 0, (dens_rows, colloc, grid_points, grid_weights, poi...  17.2 us
  transfers between devices with their start and end apart: 4, of which 4 were waited for; matrix products, arithmetic and copies ran while one was open for 1% of the time, Pallas kernels for 0%

commit v1 on v0

v1 whole, which is shorter than its diff:
```python
import functools

import jax
import jax.numpy as jnp
from jax import lax
from jax.experimental import pallas as pl
from jax.experimental.pallas import tpu as pltpu
from jax.sharding import PartitionSpec as P

SH = 64
NSIG = 16
SMEAR_SQ = 0.25
MESH = pl.DeviceIdType.MESH
F32 = jnp.float32
BF16 = jnp.bfloat16
VMEM_BYTES = 58 * 1024 * 1024


class Place:
    def __init__(self, rows, cols):
        self.n = rows // 2
        self.A = cols // self.n
        self.cols = cols
        row, col = lax.axis_index("row"), lax.axis_index("col")
        self.y, self.core = row // 2, row % 2
        self.a, self.b = col // self.n, col % self.n

    def device(self, y, core, a, b):
        return (y * 2 + core, a * self.n + b)

    def mine(self):
        return self.y, self.core, self.a, self.b

    def sides(self, core):
        return self.y * (1 - core) + self.b * core, self.b * (1 - core) + self.y * core

    def from_sides(self, core, outer, inner):
        return outer * (1 - core) + inner * core, inner * (1 - core) + outer * core

    def owner(self, y, core, a, b):
        return (y * 2 + core) * self.cols + a * self.n + b

    def greet(self):
        y, c, a, b = self.mine()
        peers = [(y, 1 - c, a, b)]
        peers += [(y, c, (a + d) % self.A, b) for d in range(1, self.A)]
        peers += [(y, c, a, (b + d) % self.n) for d in range(1, self.n)]
        peers += [((y + d) % self.n, c, a, b) for d in range(1, self.n)]
        peers += [((y + d) % self.n, 1 - c, a, b) for d in range(1, self.n)]
        barrier = pltpu.get_barrier_semaphore()
        for peer in peers:
            pl.semaphore_signal(barrier, inc=1, device_id=self.device(*peer), device_id_type=MESH)
        pl.semaphore_wait(barrier, len(peers))


def others_first(n):
    return [*range(1, n), 0]


def remote(src, dst, send_sem, recv_sem, device):
    return pltpu.make_async_remote_copy(
        src_ref=src, dst_ref=dst, send_sem=send_sem, recv_sem=recv_sem, device_id=device, device_id_type=MESH
    )


def density_kernel(
    rows, cols, occ, full, held, win, xsend, xrecv, acc, zsend, zrecv, shard,
    load_sem, wsend, wrecv, xs_sem, xr_sem, zs_sem, zr_sem, gs_sem, gr_sem, own_sem,
):
    at = Place(rows, cols)
    n, A = at.n, at.A
    y, core, a, b = at.mine()
    own_rows, slab = shard.shape
    half = slab // 2
    depth = held.shape[0]
    sibling = at.device(y, 1 - core, a, b)
    blocks = [(db, dz) for db in others_first(n) for dz in others_first(A)]

    def load(k):
        db, dz = blocks[k]
        col = (a + dz) % A * n + (b + db) % n
        start = pl.multiple_of(col * own_rows, own_rows)
        return pltpu.make_async_copy(occ.at[pl.ds(start, own_rows)], held.at[k % depth], load_sem.at[k % depth])

    for k in range(min(depth, len(blocks))):
        load(k).start()
    at.greet()

    def part(ref, h):
        return ref.at[pl.ds(h * half, half)]

    root = (y == 0) & (core == 0)
    beside = (y == 0) & (core == 1)

    def window_sends():
        sends = []
        for d in range(1, n):
            for h in range(2):
                sends.append((h, at.device((y + d) % n, h, a, b)))
        sends += [(0, sibling), (1, sibling)]
        return [
            remote(part(occ, h), part(win, h), wsend.at[i], wrecv.at[h], device)
            for i, (h, device) in enumerate(sends)
        ]

    def window_wait(h):
        remote(part(occ, h), part(win, h), wsend.at[0], wrecv.at[h], sibling).wait_recv()

    def window_forward(h):
        return remote(part(win, h), part(win, h), wsend.at[0], wrecv.at[h], sibling)

    @pl.when(root)
    def _():
        for send in window_sends():
            send.start()
        keep = pltpu.make_async_copy(occ.at[pl.ds(0, slab)], win, own_sem.at[0])
        keep.start()
        keep.wait()

    @pl.when(beside)
    def _():
        window_wait(0)
        window_wait(1)

    for h in range(2):
        @pl.when((y > 0) & (core == h))
        def _(h=h):
            window_wait(h)
            window_forward(h).start()
            window_wait(1 - h)

    tile = 512 if own_rows % 512 == 0 else own_rows

    def x_copy(db, dz):
        slot = (db - 1) * A + (a + dz) % A
        device = at.device(y, core, a, (b + db) % n)
        return remote(xsend.at[slot], xrecv.at[slot], xs_sem.at[slot], xr_sem.at[slot], device)

    for k, (db, dz) in enumerate(blocks):
        load(k).wait()
        slot = (db - 1) * A + (a + dz) % A

        @pl.loop(0, own_rows // tile)
        def _(t, k=k, db=db, dz=dz, slot=slot):
            window_rows = pl.ds(pl.multiple_of(t * tile, tile), tile)
            value = lax.dot_general(
                held[k % depth, window_rows, :], win[...], (((1,), (1,)), ((), ())), preferred_element_type=F32
            )
            if db:
                xsend[slot, window_rows, :] = value.astype(BF16)
            else:
                acc[dz, window_rows, :] = value

        if k + depth < len(blocks):
            load(k + depth).start()
        if db:
            x_copy(db, dz).start()

    def z_copy(dz):
        device = at.device(y, core, (a + dz) % A, b)
        return remote(zsend.at[dz - 1], zrecv.at[dz - 1], zs_sem.at[dz - 1], zr_sem.at[dz - 1], device)

    for dz in others_first(A):
        for db in range(1, n):
            x_copy(db, dz).wait_recv()
        total = acc[dz]
        for db in range(1, n):
            total = total + xrecv[(db - 1) * A + (a + dz) % A].astype(F32)
        if dz:
            zsend[dz - 1] = total.astype(BF16)
            z_copy(dz).start()
        else:
            acc[0] = total
    total = acc[0]
    for dz in range(1, A):
        z_copy(dz).wait_recv()
        total = total + zrecv[dz - 1].astype(F32)
    shard[...] = total.astype(BF16)

    outer, inner = at.sides(core)
    counter = [0]
    pending = []

    def rows_of(owner):
        return full.at[pl.ds(pl.multiple_of(owner * own_rows, own_rows), own_rows)]

    def forward(src, owner, device):
        i = counter[0]
        counter[0] += 1
        copy = remote(src, rows_of(owner), gs_sem.at[i], gr_sem.at[owner], device)
        copy.start()
        pending.append(copy)

    def arrived(owner):
        remote(rows_of(owner), rows_of(owner), gs_sem.at[0], gr_sem.at[owner], sibling).wait_recv()

    def owner_at(do, di, dz):
        py, pb = at.from_sides(core, (outer + do) % n, (inner + di) % n)
        return at.owner(py, core, (a + dz) % A, pb)

    def device_at(do, di, dz):
        py, pb = at.from_sides(core, (outer + do) % n, (inner + di) % n)
        return at.device(py, core, (a + dz) % A, pb)

    mine = at.owner(y, core, a, b)
    keep = pltpu.make_async_copy(shard, rows_of(mine), own_sem.at[0])
    keep.start()
    for do in range(n):
        for di in range(n):
            for dz in range(A):
                owner = owner_at(-do, -di, -dz)
                if do or di or dz:
                    arrived(owner)
                    src = rows_of(owner)
                else:
                    src = shard
                    for d in range(1, A):
                        forward(src, owner, device_at(0, 0, d))
                if not do and not di:
                    for d in range(1, n):
                        forward(src, owner, device_at(0, d, 0))
                if not do:
                    for d in range(1, n):
                        forward(src, owner, device_at(d, 0, 0))
                forward(src, owner, sibling)
    for py in range(n):
        for pb in range(n):
            for pa in range(A):
                arrived(at.owner(py, 1 - core, pa, pb))

    keep.wait()
    for copy in pending:
        copy.wait_send()
    for db, dz in blocks:
        if db:
            x_copy(db, dz).wait_send()
    for dz in range(1, A):
        z_copy(dz).wait_send()

    @pl.when(root)
    def _():
        for send in window_sends():
            send.wait_send()

    for h in range(2):
        @pl.when((y > 0) & (core == h))
        def _(h=h):
            window_forward(h).wait_send()


def gathered_density(occ_coeffs, slab):
    rows, cols = lax.axis_size("row"), lax.axis_size("col")
    n = rows // 2
    A = cols // n
    group_rows, depth = occ_coeffs.shape
    own_rows = group_rows // cols
    owners = rows * cols
    sends = A - 1 + A * (n - 1) + A * n * (n - 1) + A * n * n
    dma = pltpu.SemaphoreType.DMA
    return pl.pallas_call(
        functools.partial(density_kernel, rows, cols),
        out_shape=jax.ShapeDtypeStruct((group_rows * rows, slab), BF16),
        in_specs=[pl.BlockSpec(memory_space=pl.ANY)],
        out_specs=pl.BlockSpec(memory_space=pl.ANY),
        scratch_shapes=[
            pltpu.VMEM((4, own_rows, depth), BF16),
            pltpu.VMEM((slab, depth), BF16),
            pltpu.VMEM(((n - 1) * A, own_rows, slab), BF16),
            pltpu.VMEM(((n - 1) * A, own_rows, slab), BF16),
            pltpu.VMEM((A, own_rows, slab), F32),
            pltpu.VMEM((A - 1, own_rows, slab), BF16),
            pltpu.VMEM((A - 1, own_rows, slab), BF16),
            pltpu.VMEM((own_rows, slab), BF16),
            dma((4,)),
            dma((2 * n,)),
            dma((2,)),
            dma(((n - 1) * A,)),
            dma(((n - 1) * A,)),
            dma((A - 1,)),
            dma((A - 1,)),
            dma((sends,)),
            dma((owners,)),
            dma((1,)),
        ],
        compiler_params=pltpu.CompilerParams(
            collective_id=0, has_side_effects=True, vmem_limit_bytes=VMEM_BYTES
        ),
        name="density_everywhere",
    )(occ_coeffs)


def batch_kernel(
    lists, counts, full, colloc, points, weights, sites, proj, dense, fetched, term, fetch_sem
):
    i = pl.program_id(0)
    steps = pl.num_programs(0)
    total_points = colloc.shape[2]
    chunk = min(256, total_points)

    def fetch(step, s):
        start = pl.multiple_of(lists[step * NSIG + s] * SH, SH)
        return pltpu.make_async_copy(
            full.at[pl.ds(start, SH)], fetched.at[step % 2, pl.ds(s * SH, SH)], fetch_sem.at[step % 2, s]
        )

    @pl.when(i == 0)
    def _():
        for s in range(NSIG):
            fetch(i, s).start()
        blank = dense.shape[0] // 64

        @pl.loop(0, 64)
        def _(t):
            dense[pl.ds(pl.multiple_of(t * blank, blank), blank), :] = jnp.zeros((blank, dense.shape[1]), dense.dtype)

    @pl.when(i + 1 < steps)
    def _():
        for s in range(NSIG):
            fetch(i + 1, s).start()

    for s in range(NSIG):
        fetch(i, s).wait()
    count = counts[i]

    def point_chunk(j):
        cut = slice(j * chunk, (j + 1) * chunk)
        values = colloc[0, :, cut]
        field = lax.dot_general(
            fetched[i % 2], values, (((0,), (0,)), ((), ())), preferred_element_type=F32
        ).astype(BF16)
        projected = jnp.dot(proj[...], field, preferred_element_type=F32)
        live = (j * chunk + lax.broadcasted_iota(jnp.int32, (1, chunk), 1) < count).astype(F32)
        dist_sq = (points[0, 0:1, cut] - sites[:, 0:1]) ** 2
        dist_sq = dist_sq + (points[0, 1:2, cut] - sites[:, 1:2]) ** 2
        dist_sq = dist_sq + (points[0, 2:3, cut] - sites[:, 2:3]) ** 2
        kernel = lax.rsqrt(dist_sq + SMEAR_SQ)
        charges = (projected * kernel * (weights[0, :, cut] * live)).astype(BF16)
        spread = lax.dot_general(
            proj[...], charges, (((0,), (0,)), ((), ())), preferred_element_type=F32
        ).astype(BF16)
        return lax.dot_general(values, spread, (((1,), (1,)), ((), ())), preferred_element_type=F32)

    term[...] = point_chunk(0)
    for j in range(1, total_points // chunk):
        @pl.when(count > j * chunk)
        def _(j=j):
            term[...] += point_chunk(j)

    for s in range(NSIG):
        start = pl.multiple_of(lists[i * NSIG + s] * SH, SH)
        dense[pl.ds(start, SH), :] = term[s * SH:(s + 1) * SH, :].astype(dense.dtype)


def batch_terms(full, colloc, grid_points, grid_weights, charge_sites, charge_proj, shell_lists, point_counts):
    batches, func_rows, total_points = colloc.shape
    slab = full.shape[1]
    aux = charge_proj.shape[0]
    return pl.pallas_call(
        batch_kernel,
        out_shape=jax.ShapeDtypeStruct(full.shape, BF16),
        grid_spec=pltpu.PrefetchScalarGridSpec(
            num_scalar_prefetch=2,
            grid=(batches,),
            in_specs=[
                pl.BlockSpec(memory_space=pl.ANY),
                pl.BlockSpec((1, func_rows, total_points), lambda i, *_: (i, 0, 0)),
                pl.BlockSpec((1, 3, total_points), lambda i, *_: (i, 0, 0)),
                pl.BlockSpec((1, 1, total_points), lambda i, *_: (i, 0, 0)),
                pl.BlockSpec((aux, 3), lambda i, *_: (0, 0)),
                pl.BlockSpec((aux, slab), lambda i, *_: (0, 0)),
            ],
            out_specs=pl.BlockSpec(full.shape, lambda i, *_: (0, 0)),
            scratch_shapes=[
                pltpu.VMEM((2, func_rows, slab), BF16),
                pltpu.VMEM((func_rows, slab), F32),
                pltpu.SemaphoreType.DMA((2, NSIG)),
            ],
        ),
        compiler_params=pltpu.CompilerParams(vmem_limit_bytes=VMEM_BYTES),
        name="batch_terms",
    )(
        shell_lists.reshape(-1), point_counts, full, colloc, grid_points,
        grid_weights[:, None, :], charge_sites.T, charge_proj,
    )


def reduce_kernel(
    rows, cols, dense, out, own, r0, s1, r1, s2, r2, s3, r3,
    own_sem, s0_sem, r0_sem, s1_sem, r1_sem, s2_sem, r2_sem, s3_sem, r3_sem,
):
    at = Place(rows, cols)
    n, A = at.n, at.A
    y, core, a, b = at.mine()
    own_rows = out.shape[0]
    outer, inner = at.sides(core)
    sibling = at.device(y, 1 - core, a, b)
    order = [(do, di, dz) for do in others_first(n) for di in others_first(n) for dz in others_first(A)]

    def shard_of(side, do, di, dz):
        so, si = at.sides(side)
        py, pb = at.from_sides(side, (so + do) % n, (si + di) % n)
        pa = (a + dz) % A
        return at.owner(py, side, pa, pb), (py * A + pa) * n + pb

    def rows_of(owner):
        return dense.at[pl.ds(pl.multiple_of(owner * own_rows, own_rows), own_rows)]

    def own_load(k):
        owner, slot = shard_of(core, *order[k])
        return pltpu.make_async_copy(rows_of(owner), own.at[slot], own_sem.at[slot])

    def pair_copy(k):
        owner, slot = shard_of(1 - core, *order[k])
        return remote(rows_of(owner), r0.at[slot], s0_sem.at[slot], r0_sem.at[slot], sibling)

    def pair_wait(slot):
        remote(r0.at[slot], r0.at[slot], s0_sem.at[slot], r0_sem.at[slot], sibling).wait_recv()

    def peer(do, di, dz):
        py, pb = at.from_sides(core, (outer + do) % n, (inner + di) % n)
        return at.device(py, core, (a + dz) % A, pb)

    def outer_copy(do, di, dz):
        slot = ((do - 1) * n + (inner + di) % n) * A + (a + dz) % A
        return remote(s1.at[slot], r1.at[slot], s1_sem.at[slot], r1_sem.at[slot], peer(do, 0, 0))

    def inner_copy(di, dz):
        slot = (di - 1) * A + (a + dz) % A
        return remote(s2.at[slot], r2.at[slot], s2_sem.at[slot], r2_sem.at[slot], peer(0, di, 0))

    def last_copy(dz):
        return remote(s3.at[dz - 1], r3.at[dz - 1], s3_sem.at[dz - 1], r3_sem.at[dz - 1], peer(0, 0, dz))

    for k in range(len(order)):
        own_load(k).start()
    at.greet()
    for k in range(len(order)):
        pair_copy(k).start()

    def outer_slot(d, di, dz):
        return ((d - 1) * n + (inner + di) % n) * A + (a + dz) % A

    def inner_slot(d, dz):
        return (d - 1) * A + (a + dz) % A

    for k, (do, di, dz) in enumerate(order):
        _, slot = shard_of(core, do, di, dz)
        own_load(k).wait()
        pair_wait(slot)
        total = own[slot].astype(F32) + r0[slot].astype(F32)
        if do:
            s1[outer_slot(do, di, dz)] = total.astype(BF16)
            outer_copy(do, di, dz).start()
            continue
        for d in range(1, n):
            outer_copy(d, di, dz).wait_recv()
            total = total + r1[outer_slot(d, di, dz)].astype(F32)
        if di:
            s2[inner_slot(di, dz)] = total.astype(BF16)
            inner_copy(di, dz).start()
            continue
        for d in range(1, n):
            inner_copy(d, dz).wait_recv()
            total = total + r2[inner_slot(d, dz)].astype(F32)
        if dz:
            s3[dz - 1] = total.astype(BF16)
            last_copy(dz).start()
            continue
        for d in range(1, A):
            last_copy(d).wait_recv()
            total = total + r3[d - 1].astype(F32)
        out[...] = total

    for k, (do, di, dz) in enumerate(order):
        pair_copy(k).wait_send()
        if do:
            outer_copy(do, di, dz).wait_send()
        elif di:
            inner_copy(di, dz).wait_send()
        elif dz:
            last_copy(dz).wait_send()


def reduced_to_owners(dense):
    rows, cols = lax.axis_size("row"), lax.axis_size("col")
    n = rows // 2
    A = cols // n
    slab = dense.shape[1]
    own_rows = dense.shape[0] // (rows * cols)
    half = rows * cols // 2
    dma = pltpu.SemaphoreType.DMA

    def buffer(count):
        return pltpu.VMEM((count, own_rows, slab), BF16)

    outer, inner = (n - 1) * n * A, (n - 1) * A
    return pl.pallas_call(
        functools.partial(reduce_kernel, rows, cols),
        out_shape=jax.ShapeDtypeStruct((own_rows, slab), F32),
        in_specs=[pl.BlockSpec(memory_space=pl.ANY)],
        out_specs=pl.BlockSpec(memory_space=pltpu.VMEM),
        scratch_shapes=[
            buffer(half), buffer(half),
            buffer(outer), buffer(outer),
            buffer(inner), buffer(inner),
            buffer(A - 1), buffer(A - 1),
            dma((half,)), dma((half,)), dma((half,)),
            dma((outer,)), dma((outer,)),
            dma((inner,)), dma((inner,)),
            dma((A - 1,)), dma((A - 1,)),
        ],
        compiler_params=pltpu.CompilerParams(
            collective_id=1, has_side_effects=True, vmem_limit_bytes=VMEM_BYTES
        ),
        name="reduce_to_owners",
    )(dense)


def on_device(
    occ_coeffs, colloc, grid_points, grid_weights, charge_sites, charge_proj, shell_lists, point_counts
):
    full = gathered_density(occ_coeffs, charge_proj.shape[1])
    dense = batch_terms(
        full, colloc, grid_points, grid_weights, charge_sites, charge_proj, shell_lists, point_counts
    )
    return reduced_to_owners(dense)


def solution(mesh):
    placed = (
        P("row", "col"),
        P(("row", "col"), None, None),
        P(("row", "col"), None, None),
        P(("row", "col"), None),
        P(),
        P(),
        P(("row", "col"), None),
        P(("row", "col")),
    )
    return jax.shard_map(
        on_device, mesh=mesh, in_specs=placed, out_specs=P(("row", "col"), None), check_vma=False
    )
```

time: 608 us -> 249 us (0.41); the launches traced: 599 us -> 250 us
  waiting for transfers between devices: 413 us -> 0 us
  Pallas kernels: 0 us -> 243 us
  local copies, waits for them, and re-layouts: 78.7 us -> 7.65 us
  matrix products: 50.8 us -> 0 us
  starting transfers between devices: 14.7 us -> 0 us
  between operations: 13.5 us -> 0.03 us
  other arithmetic: 12.2 us -> 0 us
  blocking collectives: 10.7 us -> 0 us
    all_to_all x2 -> x0, waiting for transfers between devices: 274 us -> none  [the longest x1 182 us: on_device(): lax.all_to_all(tiles, ('row', 'col'), split_axis=0, concat_axis=0, tiled=...]
    pallas_call x0 -> x3, Pallas kernels: none -> 243 us  [the longest x1 130 us: gathered_density(): pl.pallas_call(functools.partial(density_kernel, rows, cols), out_shape=j...]
    reduce_scatter x1 -> x0, waiting for transfers between devices: 104 us -> none  [on_device(): lax.psum_scatter(lax.dot_general(occ_coeffs, window, (((1,), (1,)), ((),...]
    dot_general x35 -> x0, matrix products: 50.8 us -> none  [the longest x1 28.3 us: on_device(): lax.dot_general(occ_coeffs, window, (((1,), (1,)), ((), ())), preferred_e...]
    psum x1 -> x0, waiting for transfers between devices: 35.1 us -> none  [from_root(): return lax.psum(kept, axis)]
    scatter x2 -> x0, local copies, waits for them, and re-layouts: 20.6 us -> none  [the longest x1 19.6 us: on_device(): tiles = jnp.zeros((owners * capacity, SH, slab_width), jnp.float32).at[sl...]
    squeeze x16 -> x0, local copies, waits for them, and re-layouts: 18.2 us -> none  [batch_terms(): lax.scan(one_batch, 0, (dens_rows, colloc, grid_points, grid_weights, poi...]
    dynamic_slice x32 -> x0, local copies, waits for them, and re-layouts: 17.2 us -> none  [batch_terms(): lax.scan(one_batch, 0, (dens_rows, colloc, grid_points, grid_weights, poi...]
  transfers between devices with their start and end apart: 4 -> 0, of which waited for: 4 -> 0; matrix products, arithmetic and copies ran while one was open for 1% -> 0% of each run, Pallas kernels for 0% -> 0%
where the time goes in v1:
time: 249 us; the launch traced here: 250 us
  Pallas kernels  243 us (98%)
  local copies, waits for them, and re-layouts  7.65 us (3%)
    pallas_call x1, Pallas kernels, gathered_density(): pl.pallas_call(functools.partial(density_kernel, rows, cols), out_shape=j...  130 us
    pallas_call x1, Pallas kernels, reduced_to_owners(): pl.pallas_call(functools.partial(reduce_kernel, rows, cols), out_shape=ja...  88.6 us
    pallas_call x1, Pallas kernels, batch_terms(): pl.pallas_call(batch_kernel, out_shape=jax.ShapeDtypeStruct(full.shape, B...  23.9 us
    unnamed x3, local copies, waits for them, and re-layouts  5.08 us

profile of v1, /device:TPU:12, one launch (start us, length us, event | category | flops | bytes accessed | tf_op | source)
XLA Modules:
  0.0 250.4 jit_solution(6766269747334950211)
XLA Ops:
  0.0 1.2 reshape.3.lists
  1.2 1.3 broadcast_in_dim.3.weights
  2.6 1.5 copy.10.points
  4.0 1.5 copy.9
  5.6 130.2 %density_everywhere.1.full = bf16[49152,128]{1,0:T(8,128)(2,1)} custom-call(bf16[12288,2560]{1,0:T(8,128)(2,1)} %occ.1), custom_call_target="tpu_custom_call" | custom-call | tf_op jit(solution)/shard_map/density_everywhere/pallas_call | solution.py:260
  135.8 23.9 %batch_terms.1.dense = bf16[49152,128]{1,0:T(8,128)(2,1)} custom-call(s32[128]{0:T(128)} %reshape.3.lists, s32[8]{0:T(128)} %counts.1, bf16[49152,128]{1,0:T(8,128)(2,1)} %density_everywhere.1.full, bf16[8,1024,512]{2,1,0:T(8,128)(2,1)} %colloc.1, f32[8,3,512]{2,1,0:T(4,128)} %copy.10.points, f32[8,1,512]{2,1,0:T(1,128)} %broadcast_in_dim.3.weights, ...), custom_call_target="tpu_custom_call" | custom-call | tf_op jit(solution)/shard_map/batch_terms/pallas_call | solution.py:358
  159.7 88.6 %reduce_to_owners.1 = f32[1536,128]{1,0:T(8,128)} custom-call(bf16[49152,128]{1,0:T(8,128)(2,1)} %batch_terms.1.dense), custom_call_target="tpu_custom_call" | custom-call | tf_op jit(solution)/shard_map/reduce_to_owners/pallas_call | solution.py:497
  248.3 2.1 copy.12

commit v2 on v1

v2 whole, which is shorter than its diff:
```python
import functools

import jax
import jax.numpy as jnp
from jax import lax
from jax.experimental import pallas as pl
from jax.experimental.pallas import tpu as pltpu
from jax.sharding import PartitionSpec as P

SH = 64
NSIG = 16
SMEAR_SQ = 0.25
MESH = pl.DeviceIdType.MESH
F32 = jnp.float32
BF16 = jnp.bfloat16
VMEM_BYTES = 58 * 1024 * 1024
HELD = 12


class Place:
    def __init__(self, rows, cols):
        self.n = rows // 2
        self.A = cols // self.n
        self.cols = cols
        row, col = lax.axis_index("row"), lax.axis_index("col")
        self.y, self.core = row // 2, row % 2
        self.a, self.b = col // self.n, col % self.n

    def device(self, y, core, a, b):
        return (y * 2 + core, a * self.n + b)

    def mine(self):
        return self.y, self.core, self.a, self.b

    def sides(self, core):
        return self.y * (1 - core) + self.b * core, self.b * (1 - core) + self.y * core

    def from_sides(self, core, outer, inner):
        return outer * (1 - core) + inner * core, inner * (1 - core) + outer * core

    def owner(self, y, core, a, b):
        return (y * 2 + core) * self.cols + a * self.n + b

    def greet(self):
        y, c, a, b = self.mine()
        peers = [(y, 1 - c, a, b)]
        peers += [(y, c, (a + d) % self.A, b) for d in range(1, self.A)]
        peers += [(y, c, a, (b + d) % self.n) for d in range(1, self.n)]
        peers += [((y + d) % self.n, c, a, b) for d in range(1, self.n)]
        peers += [((y + d) % self.n, 1 - c, a, b) for d in range(1, self.n)]
        barrier = pltpu.get_barrier_semaphore()
        for peer in peers:
            pl.semaphore_signal(barrier, inc=1, device_id=self.device(*peer), device_id_type=MESH)
        pl.semaphore_wait(barrier, len(peers))


def others_first(n):
    return [*range(1, n), 0]


def remote(src, dst, send_sem, recv_sem, device):
    return pltpu.make_async_remote_copy(
        src_ref=src, dst_ref=dst, send_sem=send_sem, recv_sem=recv_sem, device_id=device, device_id_type=MESH
    )


def density_kernel(
    rows, cols, occ, full, held, win, xsend, xrecv, acc, zsend, zrecv, shard,
    load_sem, wsend, wrecv, xs_sem, xr_sem, zs_sem, zr_sem, gu_sem, gd_sem, gi_sem, go_sem, gp_sem, gr_sem, own_sem,
):
    at = Place(rows, cols)
    n, A = at.n, at.A
    y, core, a, b = at.mine()
    own_rows, slab = shard.shape
    half = slab // 2
    depth = held.shape[0]
    sibling = at.device(y, 1 - core, a, b)
    parts = parts_of(own_rows)
    sub = own_rows // parts
    per = n * A
    steps = parts * per

    def block(k):
        j = k % per
        return k // per, (j // A + 1) % n, (j + 1) % A

    def load(k):
        s, db, dz = block(k)
        col = (a + dz) % A * n + (b + db) % n
        start = pl.multiple_of(col * own_rows + s * sub, sub)
        return pltpu.make_async_copy(occ.at[pl.ds(start, sub)], held.at[k % depth], load_sem.at[k % depth])

    for k in range(min(depth, steps)):
        load(k).start()
    at.greet()

    def part(ref, h):
        return ref.at[pl.ds(h * half, half)]

    root = (y == 0) & (core == 0)
    beside = (y == 0) & (core == 1)

    def window_sends():
        sends = []
        for d in range(1, n):
            for h in range(2):
                sends.append((h, at.device((y + d) % n, h, a, b)))
        sends += [(0, sibling), (1, sibling)]
        return [
            remote(part(occ, h), part(win, h), wsend.at[i], wrecv.at[h], device)
            for i, (h, device) in enumerate(sends)
        ]

    def window_wait(h):
        remote(part(occ, h), part(win, h), wsend.at[0], wrecv.at[h], sibling).wait_recv()

    def window_forward(h):
        return remote(part(win, h), part(win, h), wsend.at[0], wrecv.at[h], sibling)

    @pl.when(root)
    def _():
        for send in window_sends():
            send.start()
        keep = pltpu.make_async_copy(occ.at[pl.ds(0, slab)], win, own_sem.at[0])
        keep.start()
        keep.wait()

    @pl.when(beside)
    def _():
        window_wait(0)
        window_wait(1)

    for h in range(2):
        @pl.when((y > 0) & (core == h))
        def _(h=h):
            window_wait(h)
            window_forward(h).start()
            window_wait(1 - h)

    def rows_in(s):
        return pl.ds(s * sub, sub)

    def x_slot(db, dz):
        return (db - 1) * A + (a + dz) % A

    def x_copy(s, db, dz):
        slot = x_slot(db, dz)
        device = at.device(y, core, a, (b + db) % n)
        return remote(
            xsend.at[slot, rows_in(s)], xrecv.at[slot, rows_in(s)], xs_sem.at[slot, s], xr_sem.at[slot, s], device
        )

    def z_copy(s, dz):
        device = at.device(y, core, (a + dz) % A, b)
        return remote(
            zsend.at[dz - 1, rows_in(s)], zrecv.at[dz - 1, rows_in(s)],
            zs_sem.at[dz - 1, s], zr_sem.at[dz - 1, s], device,
        )

    def product(k):
        load(k).wait()
        value = lax.dot_general(
            held[k % depth], win[...], (((1,), (1,)), ((), ())), preferred_element_type=F32
        )
        return value

    def refill(k):
        @pl.when(k + depth < steps)
        def _():
            load(k + depth).start()

    def send_products(s):
        @pl.loop(s * per, s * per + per - A)
        def _(k):
            _, db, dz = block(k)
            xsend[x_slot(db, dz), rows_in(s), :] = product(k).astype(BF16)
            x_copy(s, db, dz).start()
            refill(k)

    def keep_products(s):
        @pl.loop(s * per + per - A, s * per + per)
        def _(k):
            _, _, dz = block(k)
            acc[dz, rows_in(s), :] = product(k)
            refill(k)

    def sum_b(s):
        for dz in others_first(A):
            for db in range(1, n):
                x_copy(s, db, dz).wait_recv()
            total = acc[dz, rows_in(s), :]
            for db in range(1, n):
                total = total + xrecv[x_slot(db, dz), rows_in(s), :].astype(F32)
            if dz:
                zsend[dz - 1, rows_in(s), :] = total.astype(BF16)
                z_copy(s, dz).start()
            else:
                acc[0, rows_in(s), :] = total

    outer, inner = at.sides(core)

    def rows_of(s, owner):
        return full.at[pl.ds(pl.multiple_of(owner * own_rows + s * sub, sub), sub)]

    def copy_of(src, s, owner, sems, i, device):
        return remote(src, rows_of(s, owner), sems.at[s, i], gr_sem.at[owner, s], device)

    def arrived(s, owner):
        copy_of(rows_of(s, owner), s, owner, gp_sem, 0, sibling).wait_recv()

    def shard_at(do, di, pa):
        py, pb = at.from_sides(core, (outer + do) % n, (inner + di) % n)
        return at.owner(py, core, pa, pb)

    def device_at(do, di, pa):
        py, pb = at.from_sides(core, (outer + do) % n, (inner + di) % n)
        return at.device(py, core, pa, pb)

    def to_sibling(src, s, do, di, pa):
        return copy_of(src, s, shard_at(-do, -di, pa), gp_sem, (do * n + di) * A + pa, sibling)

    def to_outer(src, s, di, pa):
        return [
            copy_of(src, s, shard_at(0, -di, pa), go_sem, ((d - 1) * n + di) * A + pa, device_at(d, 0, a))
            for d in range(1, n)
        ]

    def to_inner(src, s, pa):
        return [
            copy_of(src, s, shard_at(0, 0, pa), gi_sem, (d - 1) * A + pa, device_at(0, d, a))
            for d in range(1, n)
        ]

    def to_up(src, s, pa):
        return copy_of(src, s, shard_at(0, 0, pa), gu_sem, pa, at.device(y, core, (a + 1) % A, b))

    def to_down(src, s, pa):
        return copy_of(src, s, shard_at(0, 0, pa), gd_sem, pa, at.device(y, core, (a + A - 1) % A, b))

    mine = at.owner(y, core, a, b)

    def keep_copy(s):
        return pltpu.make_async_copy(shard.at[rows_in(s)], rows_of(s, mine), own_sem.at[s])

    def finish(s):
        total = acc[0, rows_in(s), :]
        for dz in range(1, A):
            z_copy(s, dz).wait_recv()
            total = total + zrecv[dz - 1, rows_in(s), :].astype(F32)
        shard[rows_in(s), :] = total.astype(BF16)
        own = shard.at[rows_in(s)]

        @pl.when(a < A - 1)
        def _():
            to_up(own, s, a).start()

        @pl.when(a > 0)
        def _():
            to_down(own, s, a).start()

        for copy in to_outer(own, s, 0, a) + to_inner(own, s, a):
            copy.start()
        to_sibling(own, s, 0, 0, a).start()
        keep_copy(s).start()

    def along_a(s, j):
        def pass_on(pa, further, send):
            owner = shard_at(0, 0, pa)
            arrived(s, owner)
            src = rows_of(s, owner)

            @pl.when(further)
            def _():
                send(src, s, pa).start()

            for copy in to_outer(src, s, 0, pa) + to_inner(src, s, pa):
                copy.start()
            to_sibling(src, s, 0, 0, pa).start()

        @pl.when(a - j >= 0)
        def _():
            pass_on(a - j, a < A - 1, to_up)

        @pl.when(a + j < A)
        def _():
            pass_on(a + j, a > 0, to_down)

    def along_inner(s):
        for dz in near_first:
            for di in range(1, n):
                pa = (a + dz) % A
                owner = shard_at(0, -di, pa)
                arrived(s, owner)
                for copy in to_outer(rows_of(s, owner), s, di, pa):
                    copy.start()
                to_sibling(rows_of(s, owner), s, 0, di, pa).start()

    def along_outer(s):
        for di in range(n):
            for dz in near_first:
                for do in range(1, n):
                    pa = (a + dz) % A
                    owner = shard_at(-do, -di, pa)
                    arrived(s, owner)
                    to_sibling(rows_of(s, owner), s, do, di, pa).start()

    near_first = sorted(range(A), key=lambda d: min(d, A - d))

    def stage(name, s):
        if 0 <= s < parts:
            name(s)

    def spread_a(s):
        for j in range(1, A):
            along_a(s, j)

    for s in range(parts + 5):
        stage(send_products, s)
        stage(sum_b, s - 1)
        stage(keep_products, s)
        stage(finish, s - 2)
        stage(spread_a, s - 3)
        stage(along_inner, s - 3)
        stage(along_outer, s - 4)

    for s in range(parts):
        @pl.loop(0, n * A * n)
        def _(q, s=s):
            py, pa, pb = q // (A * n), q // n % A, q % n
            arrived(s, at.owner(py, 1 - core, pa, pb))

    for s in range(parts):
        keep_copy(s).wait()

        @pl.loop(0, A)
        def _(pa, s=s):
            src = shard.at[rows_in(s)]

            @pl.when((pa <= a) & (a < A - 1))
            def _():
                to_up(src, s, pa).wait_send()

            @pl.when((pa >= a) & (a > 0))
            def _():
                to_down(src, s, pa).wait_send()

            for copy in to_inner(src, s, pa):
                copy.wait_send()
            for di in range(n):
                for copy in to_outer(src, s, di, pa):
                    copy.wait_send()
                for do in range(n):
                    to_sibling(src, s, do, di, pa).wait_send()
            for db in range(1, n):
                x_copy(s, db, (pa + A - a) % A).wait_send()

        for dz in range(1, A):
            z_copy(s, dz).wait_send()

    @pl.when(root)
    def _():
        for send in window_sends():
            send.wait_send()

    for h in range(2):
        @pl.when((y > 0) & (core == h))
        def _(h=h):
            window_forward(h).wait_send()


def parts_of(own_rows):
    return next(parts for parts in (3, 2, 1) if own_rows % (parts * 16) == 0)


def gathered_density(occ_coeffs, slab):
    rows, cols = lax.axis_size("row"), lax.axis_size("col")
    n = rows // 2
    A = cols // n
    group_rows, depth = occ_coeffs.shape
    own_rows = group_rows // cols
    owners = rows * cols
    parts = parts_of(own_rows)
    side = (n - 1) * A
    dma = pltpu.SemaphoreType.DMA
    return pl.pallas_call(
        functools.partial(density_kernel, rows, cols),
        out_shape=jax.ShapeDtypeStruct((group_rows * rows, slab), BF16),
        in_specs=[pl.BlockSpec(memory_space=pl.ANY)],
        out_specs=pl.BlockSpec(memory_space=pl.ANY),
        scratch_shapes=[
            pltpu.VMEM((HELD, own_rows // parts, depth), BF16),
            pltpu.VMEM((slab, depth), BF16),
            pltpu.VMEM(((n - 1) * A, own_rows, slab), BF16),
            pltpu.VMEM(((n - 1) * A, own_rows, slab), BF16),
            pltpu.VMEM((A, own_rows, slab), F32),
            pltpu.VMEM((A - 1, own_rows, slab), BF16),
            pltpu.VMEM((A - 1, own_rows, slab), BF16),
            pltpu.VMEM((own_rows, slab), BF16),
            dma((HELD,)),
            dma((2 * n,)),
            dma((2,)),
            dma((side, parts)),
            dma((side, parts)),
            dma((A - 1, parts)),
            dma((A - 1, parts)),
            dma((parts, A)),
            dma((parts, A)),
            dma((parts, side)),
            dma((parts, side * n)),
            dma((parts, A * n * n)),
            dma((owners, parts)),
            dma((parts,)),
        ],
        compiler_params=pltpu.CompilerParams(
            collective_id=0, has_side_effects=True, vmem_limit_bytes=VMEM_BYTES
        ),
        name="density_everywhere",
    )(occ_coeffs)


def batch_kernel(
    lists, counts, full, colloc, points, weights, charge_sites, proj, dense, fetched, term, rows, sites, fetch_sem
):
    i = pl.program_id(0)
    steps = pl.num_programs(0)
    total_points = colloc.shape[2]
    chunk = min(256, total_points)

    def fetch(step, s):
        start = pl.multiple_of(lists[step, s] * SH, SH)
        return pltpu.make_async_copy(
            full.at[pl.ds(start, SH)], fetched.at[step % 2, pl.ds(s * SH, SH)], fetch_sem.at[step % 2, s]
        )

    @pl.when(i == 0)
    def _():
        for s in range(NSIG):
            fetch(i, s).start()
        rows[...] = jnp.zeros(rows.shape, F32)
        rows[0:3, :] = charge_sites[...]
        sites[...] = rows[...].T
        blank = dense.shape[0] // 64

        @pl.loop(0, 64)
        def _(t):
            dense[pl.ds(pl.multiple_of(t * blank, blank), blank), :] = jnp.zeros((blank, dense.shape[1]), dense.dtype)

    @pl.when(i + 1 < steps)
    def _():
        for s in range(NSIG):
            fetch(i + 1, s).start()

    for s in range(NSIG):
        fetch(i, s).wait()
    count = counts[i]

    def point_chunk(j):
        cut = slice(j * chunk, (j + 1) * chunk)
        values = colloc[0, :, cut]
        field = lax.dot_general(
            fetched[i % 2], values, (((0,), (0,)), ((), ())), preferred_element_type=F32
        ).astype(BF16)
        projected = jnp.dot(proj[...], field, preferred_element_type=F32)
        live = (j * chunk + lax.broadcasted_iota(jnp.int32, (1, chunk), 1) < count).astype(F32)
        dist_sq = (points[0, 0:1, cut] - sites[:, 0:1]) ** 2
        dist_sq = dist_sq + (points[0, 1:2, cut] - sites[:, 1:2]) ** 2
        dist_sq = dist_sq + (points[0, 2:3, cut] - sites[:, 2:3]) ** 2
        kernel = lax.rsqrt(dist_sq + SMEAR_SQ)
        charges = (projected * kernel * (weights[pl.ds(i, 1), cut] * live)).astype(BF16)
        spread = lax.dot_general(
            proj[...], charges, (((0,), (0,)), ((), ())), preferred_element_type=F32
        ).astype(BF16)
        return lax.dot_general(values, spread, (((1,), (1,)), ((), ())), preferred_element_type=F32)

    term[...] = point_chunk(0)
    for j in range(1, total_points // chunk):
        @pl.when(count > j * chunk)
        def _(j=j):
            term[...] += point_chunk(j)

    for s in range(NSIG):
        start = pl.multiple_of(lists[i, s] * SH, SH)
        dense[pl.ds(start, SH), :] = term[s * SH:(s + 1) * SH, :].astype(dense.dtype)


def batch_terms(full, colloc, grid_points, grid_weights, charge_sites, charge_proj, shell_lists, point_counts):
    batches, func_rows, total_points = colloc.shape
    slab = full.shape[1]
    aux = charge_proj.shape[0]
    return pl.pallas_call(
        batch_kernel,
        out_shape=jax.ShapeDtypeStruct(full.shape, BF16),
        grid_spec=pltpu.PrefetchScalarGridSpec(
            num_scalar_prefetch=2,
            grid=(batches,),
            in_specs=[
                pl.BlockSpec(memory_space=pl.ANY),
                pl.BlockSpec((1, func_rows, total_points), lambda i, *_: (i, 0, 0)),
                pl.BlockSpec((1, 3, total_points), lambda i, *_: (i, 0, 0)),
                pl.BlockSpec((batches, total_points), lambda i, *_: (0, 0)),
                pl.BlockSpec((3, aux), lambda i, *_: (0, 0)),
                pl.BlockSpec((aux, slab), lambda i, *_: (0, 0)),
            ],
            out_specs=pl.BlockSpec(full.shape, lambda i, *_: (0, 0)),
            scratch_shapes=[
                pltpu.VMEM((2, func_rows, slab), BF16),
                pltpu.VMEM((func_rows, slab), F32),
                pltpu.VMEM((8, aux), F32),
                pltpu.VMEM((aux, 8), F32),
                pltpu.SemaphoreType.DMA((2, NSIG)),
            ],
        ),
        compiler_params=pltpu.CompilerParams(vmem_limit_bytes=VMEM_BYTES),
        name="batch_terms",
    )(
        shell_lists, point_counts, full, colloc, grid_points,
        grid_weights, charge_sites, charge_proj,
    )


def reduce_kernel(
    rows, cols, dense, out, own, r0, s1, r1, s2, r2, s3, r3,
    own_sem, s0_sem, r0_sem, s1_sem, r1_sem, s2_sem, r2_sem, s3_sem, r3_sem,
):
    at = Place(rows, cols)
    n, A = at.n, at.A
    y, core, a, b = at.mine()
    own_rows = out.shape[0]
    outer, inner = at.sides(core)
    sibling = at.device(y, 1 - core, a, b)
    order = [(do, di, dz) for do in others_first(n) for di in others_first(n) for dz in others_first(A)]

    def shard_of(side, do, di, dz):
        so, si = at.sides(side)
        py, pb = at.from_sides(side, (so + do) % n, (si + di) % n)
        pa = (a + dz) % A
        return at.owner(py, side, pa, pb), (py * A + pa) * n + pb

    parts = parts_of(own_rows)
    sub = own_rows // parts

    def rows_of(owner, s):
        return dense.at[pl.ds(pl.multiple_of(owner * own_rows + s * sub, sub), sub)]

    def rows_in(s):
        return pl.ds(s * sub, sub)

    def own_load(k, s):
        owner, slot = shard_of(core, *order[k])
        return pltpu.make_async_copy(rows_of(owner, s), own.at[slot, rows_in(s)], own_sem.at[slot, s])

    def pair_copy(k, s):
        owner, slot = shard_of(1 - core, *order[k])
        return remote(
            rows_of(owner, s), r0.at[slot, rows_in(s)], s0_sem.at[slot, s], r0_sem.at[slot, s], sibling
        )

    def pair_wait(slot, s):
        there = r0.at[slot, rows_in(s)]
        remote(there, there, s0_sem.at[slot, s], r0_sem.at[slot, s], sibling).wait_recv()

    def peer(do, di, dz):
        py, pb = at.from_sides(core, (outer + do) % n, (inner + di) % n)
        return at.device(py, core, (a + dz) % A, pb)

    def outer_slot(do, di, dz):
        return ((do - 1) * n + (inner + di) % n) * A + (a + dz) % A

    def inner_slot(di, dz):
        return (di - 1) * A + (a + dz) % A

    def slot_copy(src, dst, src_sem, dst_sem, slot, s, device):
        return remote(
            src.at[slot, rows_in(s)], dst.at[slot, rows_in(s)], src_sem.at[slot, s], dst_sem.at[slot, s], device
        )

    def outer_copy(do, di, dz, s):
        return slot_copy(s1, r1, s1_sem, r1_sem, outer_slot(do, di, dz), s, peer(do, 0, 0))

    def inner_copy(di, dz, s):
        return slot_copy(s2, r2, s2_sem, r2_sem, inner_slot(di, dz), s, peer(0, di, 0))

    def last_copy(dz, s):
        return slot_copy(s3, r3, s3_sem, r3_sem, dz - 1, s, peer(0, 0, dz))

    for s in range(parts):
        for k in range(len(order)):
            own_load(k, s).start()
    at.greet()
    for s in range(parts):
        for k in range(len(order)):
            pair_copy(k, s).start()

    def add_up(k, s):
        do, di, dz = order[k]
        _, slot = shard_of(core, do, di, dz)
        rows = rows_in(s)
        own_load(k, s).wait()
        pair_wait(slot, s)
        total = own[slot, rows, :].astype(F32) + r0[slot, rows, :].astype(F32)
        if do:
            s1[outer_slot(do, di, dz), rows, :] = total.astype(BF16)
            outer_copy(do, di, dz, s).start()
            return
        for d in range(1, n):
            outer_copy(d, di, dz, s).wait_recv()
            total = total + r1[outer_slot(d, di, dz), rows, :].astype(F32)
        if di:
            s2[inner_slot(di, dz), rows, :] = total.astype(BF16)
            inner_copy(di, dz, s).start()
            return
        for d in range(1, n):
            inner_copy(d, dz, s).wait_recv()
            total = total + r2[inner_slot(d, dz), rows, :].astype(F32)
        if dz:
            s3[dz - 1, rows, :] = total.astype(BF16)
            last_copy(dz, s).start()
            return
        for d in range(1, A):
            last_copy(d, s).wait_recv()
            total = total + r3[d - 1, rows, :].astype(F32)
        out[rows, :] = total

    def level(place):
        do, di, dz = place
        return 0 if do else 1 if di else 2 if dz else 3

    for step in range(parts + 3):
        for stage in range(4):
            s = step - stage
            if 0 <= s < parts:
                for k, place in enumerate(order):
                    if level(place) == stage:
                        add_up(k, s)

    for s in range(parts):
        for k, (do, di, dz) in enumerate(order):
            pair_copy(k, s).wait_send()
            if do:
                outer_copy(do, di, dz, s).wait_send()
            elif di:
                inner_copy(di, dz, s).wait_send()
            elif dz:
                last_copy(dz, s).wait_send()


def reduced_to_owners(dense):
    rows, cols = lax.axis_size("row"), lax.axis_size("col")
    n = rows // 2
    A = cols // n
    slab = dense.shape[1]
    own_rows = dense.shape[0] // (rows * cols)
    half = rows * cols // 2
    parts = parts_of(own_rows)
    dma = pltpu.SemaphoreType.DMA

    def buffer(count):
        return pltpu.VMEM((count, own_rows, slab), BF16)

    outer, inner = (n - 1) * n * A, (n - 1) * A
    return pl.pallas_call(
        functools.partial(reduce_kernel, rows, cols),
        out_shape=jax.ShapeDtypeStruct((own_rows, slab), F32),
        in_specs=[pl.BlockSpec(memory_space=pl.ANY)],
        out_specs=pl.BlockSpec(memory_space=pltpu.VMEM),
        scratch_shapes=[
            buffer(half), buffer(half),
            buffer(outer), buffer(outer),
            buffer(inner), buffer(inner),
            buffer(A - 1), buffer(A - 1),
            dma((half, parts)), dma((half, parts)), dma((half, parts)),
            dma((outer, parts)), dma((outer, parts)),
            dma((inner, parts)), dma((inner, parts)),
            dma((A - 1, parts)), dma((A - 1, parts)),
        ],
        compiler_params=pltpu.CompilerParams(
            collective_id=1, has_side_effects=True, vmem_limit_bytes=VMEM_BYTES
        ),
        name="reduce_to_owners",
    )(dense)


def on_device(
    occ_coeffs, colloc, grid_points, grid_weights, charge_sites, charge_proj, shell_lists, point_counts
):
    full = gathered_density(occ_coeffs, charge_proj.shape[1])
    dense = batch_terms(
        full, colloc, grid_points, grid_weights, charge_sites, charge_proj, shell_lists, point_counts
    )
    return reduced_to_owners(dense)


def solution(mesh):
    placed = (
        P("row", "col"),
        P(("row", "col"), None, None),
        P(("row", "col"), None, None),
        P(("row", "col"), None),
        P(),
        P(),
        P(("row", "col"), None),
        P(("row", "col")),
    )
    return jax.shard_map(
        on_device, mesh=mesh, in_specs=placed, out_specs=P(("row", "col"), None), check_vma=False
    )
```

time: 249 us -> 216 us (0.87)
  the two profiles are of different devices: /device:TPU:12 before, /device:TPU:8 now
where the time goes in v2:
time: 216 us; the launch traced here: 212 us
  Pallas kernels  209 us (97%)
  local copies, waits for them, and re-layouts  3.53 us (2%)
    pallas_call x1, Pallas kernels, gathered_density(): pl.pallas_call(functools.partial(density_kernel, rows, cols), out_shape=j...  110 us
    pallas_call x1, Pallas kernels, reduced_to_owners(): pl.pallas_call(functools.partial(reduce_kernel, rows, cols), out_shape=ja...  80.2 us
    pallas_call x1, Pallas kernels, batch_terms(): pl.pallas_call(batch_kernel, out_shape=jax.ShapeDtypeStruct(full.shape, B...  18.1 us

profile of v2, /device:TPU:8, one launch (start us, length us, event | category | flops | bytes accessed | tf_op | source)
XLA Modules:
  0.0 212.3 jit_solution(8364135904409468946)
XLA Ops:
  0.0 1.5 copy.9.points
  1.5 110.5 %density_everywhere.1.full = bf16[49152,128]{1,0:T(8,128)(2,1)} custom-call(bf16[12288,2560]{1,0:T(8,128)(2,1)} %occ.1), custom_call_target="tpu_custom_call" | custom-call | tf_op jit(solution)/shard_map/density_everywhere/pallas_call | solution.py:385
  112.0 18.1 %batch_terms.1.dense = bf16[49152,128]{1,0:T(8,128)(2,1)} custom-call(s32[8,16]{1,0:T(8,128)} %lists.1, s32[8]{0:T(128)} %counts.1, bf16[49152,128]{1,0:T(8,128)(2,1)} %density_everywhere.1.full, bf16[8,1024,512]{2,1,0:T(8,128)(2,1)} %colloc.1, f32[8,3,512]{2,1,0:T(4,128)} %copy.9.points, f32[8,512]{1,0:T(8,128)} %weights.1, f32[3,512]{1,0:T(4,128)} %charge_sites.1, ...), custom_call_target="tpu_custom_call" | custom-call | tf_op jit(solution)/shard_map/batch_terms/pallas_call | solution.py:490
  130.0 80.2 %reduce_to_owners.1 = f32[1536,128]{1,0:T(8,128)} custom-call(bf16[49152,128]{1,0:T(8,128)(2,1)} %batch_terms.1.dense), custom_call_target="tpu_custom_call" | custom-call | tf_op jit(solution)/shard_map/reduce_to_owners/pallas_call | solution.py:661
  210.2 2.1 copy.11

commit v3 on v2

--- a/solution.py
+++ b/solution.py
@@ -14,7 +14,7 @@
 F32 = jnp.float32
 BF16 = jnp.bfloat16
 VMEM_BYTES = 58 * 1024 * 1024
-HELD = 12
+HELD = 16
 
 
 class Place:
@@ -369,7 +369,7 @@
 
 
 def parts_of(own_rows):
-    return next(parts for parts in (3, 2, 1) if own_rows % (parts * 16) == 0)
+    return next(parts for parts in (4, 3, 2, 1) if own_rows % (parts * 16) == 0)
 
 
 def gathered_density(occ_coeffs, slab):

time: 216 us -> 209 us (0.968)
  the two profiles are of different devices: /device:TPU:8 before, /device:TPU:12 now
where the time goes in v3:
time: 209 us; the launch traced here: 206 us
  Pallas kernels  203 us (97%)
  local copies, waits for them, and re-layouts  3.53 us (2%)
    pallas_call x1, Pallas kernels, gathered_density(): pl.pallas_call(functools.partial(density_kernel, rows, cols), out_shape=j...  107 us
    pallas_call x1, Pallas kernels, reduced_to_owners(): pl.pallas_call(functools.partial(reduce_kernel, rows, cols), out_shape=ja...  78.1 us
    pallas_call x1, Pallas kernels, batch_terms(): pl.pallas_call(batch_kernel, out_shape=jax.ShapeDtypeStruct(full.shape, B...  18.1 us

profile of v3, /device:TPU:12, one launch (start us, length us, event | category | flops | bytes accessed | tf_op | source)
XLA Modules:
  0.0 206.5 jit_solution(9239749076307840261)
XLA Ops:
  0.0 1.5 copy.9.points
  1.5 106.7 %density_everywhere.1.full = bf16[49152,128]{1,0:T(8,128)(2,1)} custom-call(bf16[12288,2560]{1,0:T(8,128)(2,1)} %occ.1), custom_call_target="tpu_custom_call" | custom-call | tf_op jit(solution)/shard_map/density_everywhere/pallas_call | solution.py:385
  108.2 18.1 %batch_terms.1.dense = bf16[49152,128]{1,0:T(8,128)(2,1)} custom-call(s32[8,16]{1,0:T(8,128)} %lists.1, s32[8]{0:T(128)} %counts.1, bf16[49152,128]{1,0:T(8,128)(2,1)} %density_everywhere.1.full, bf16[8,1024,512]{2,1,0:T(8,128)(2,1)} %colloc.1, f32[8,3,512]{2,1,0:T(4,128)} %copy.9.points, f32[8,512]{1,0:T(8,128)} %weights.1, f32[3,512]{1,0:T(4,128)} %charge_sites.1, ...), custom_call_target="tpu_custom_call" | custom-call | tf_op jit(solution)/shard_map/batch_terms/pallas_call | solution.py:490
  126.3 78.1 %reduce_to_owners.1 = f32[1536,128]{1,0:T(8,128)} custom-call(bf16[49152,128]{1,0:T(8,128)(2,1)} %batch_terms.1.dense), custom_call_target="tpu_custom_call" | custom-call | tf_op jit(solution)/shard_map/reduce_to_owners/pallas_call | solution.py:661
  204.4 2.1 copy.11
